TPU v7x, 32 devices: a whole 2x2x4 slice. The times are simulated.
32 devices in a mesh: grp: 2 (over y), ep: 4 (over z), dp: 4 (over x, core).
Axes of the slice: x: 2, y: 2, z: 4, core: 2. Of those that a mesh axis runs over, the one named last changes fastest.
Arguments:
- tokens: bfloat16 [128, 7168], P(('grp', 'ep', 'dp')), parts along dimension 0, may hold values from -6 to 6
- expert_ids: int32 [128, 8], P(('grp', 'ep', 'dp')), parts along dimension 0, may hold values from 0 to 15, all different within a row; in each aligned block of 4 rows (0 to 3, 4 to 7, ...) at most 3 rows name the same one
- combine_weight: float32 [128, 8], P(('grp', 'ep', 'dp')), parts along dimension 0, may hold values from 0.1 to 1
- slot_of_expert: int32 [16], replicated, may hold values from 0 to 15, each once
- w_gate: bfloat16 [16, 7168, 2048], P('ep', None, 'dp'), may hold values from -0.0625 to 0.0625
- w_up: bfloat16 [16, 7168, 2048], P('ep', None, 'dp'), may hold values from -0.0625 to 0.0625
- w_down: bfloat16 [16, 2048, 7168], P('ep', 'dp'), may hold values from -0.125 to 0.125
Outputs:
- mixed: bfloat16 [128, 7168], P(('grp', 'ep', 'dp')), parts along dimension 0
There are 2 independent parts, one for each index of `grp`. A program takes and returns all parts, laid end to end along the dimension named above; an argument that names none is the same for every part. Nothing has to cross between parts.
Inputs may be any that keep to these rules, and one draw needn't show every extreme that they name: `expert_ids`: among the rows of one device no expert is named by more than 3 rows. `slot_of_expert`: every stored slot serves exactly one expert.
All inputs are finite; a program needn't handle non-finite values.
Results may differ from a plain program's by a relative error of at most 0.015.
Values may be sent and summed in bfloat16 or wider, within the bound.
A program may use at most 128 MiB of HBM per device.

v0:
```python
import jax
import jax.numpy as jnp
from jax import lax
from jax.sharding import PartitionSpec as P

TOP = 8
EXPERTS = 16
CAP = 3


def route_select(expert_ids, slot_of_expert):
    rows = expert_ids.shape[0]
    numbers = jnp.arange(EXPERTS, dtype=jnp.int32)
    chosen = (expert_ids.reshape(-1)[:, None] == numbers[None, :]).astype(jnp.int32)
    picked = jnp.sum(chosen * slot_of_expert[None, :], axis=1)
    member = (picked[:, None] == numbers[None, :]).astype(jnp.int32)
    before = jnp.cumsum(member, axis=0) - member
    position = jnp.sum(before * member, axis=1)
    target = picked * CAP + position
    places = jnp.arange(EXPERTS * CAP, dtype=jnp.int32)
    select = (target[:, None] == places[None, :]).astype(jnp.float32)
    return select.reshape(rows, TOP, EXPERTS * CAP)


def expert_rows(piece, w_gate, w_up, w_down):
    gate = jnp.einsum("kpjcd,jdf->kpjcf", piece, w_gate, preferred_element_type=jnp.float32)
    upper = jnp.einsum("kpjcd,jdf->kpjcf", piece, w_up, preferred_element_type=jnp.float32)
    hidden = (jax.nn.silu(gate) * upper).astype(jnp.bfloat16)
    return jnp.einsum("kpjcf,jfd->kpjcd", hidden, w_down, preferred_element_type=jnp.float32)


def body(tokens, expert_ids, combine_weight, slot_of_expert, w_gate, w_up, w_down):
    ep_count = lax.axis_size("ep")
    local_slots = w_gate.shape[0]
    width = tokens.shape[1]
    select = route_select(expert_ids, slot_of_expert)
    combine = jnp.einsum("tke,tk->te", select, combine_weight)
    dispatch = jnp.transpose(jnp.sum(select, axis=1)).astype(jnp.bfloat16)
    outgoing = jnp.dot(dispatch, tokens, preferred_element_type=jnp.float32).astype(jnp.bfloat16)
    outgoing = outgoing.reshape(ep_count, local_slots, CAP, width)
    arrived = lax.all_to_all(outgoing, "ep", split_axis=0, concat_axis=0, tiled=True)
    partial_value = expert_rows(
        lax.all_gather(arrived[None], "dp", axis=0, tiled=True), w_gate, w_up, w_down
    )
    summed = lax.psum_scatter(
        partial_value.astype(jnp.bfloat16), "dp", scatter_dimension=0, tiled=True
    )
    returned = lax.all_to_all(summed, "ep", split_axis=1, concat_axis=1, tiled=True)
    expert_out = returned.reshape(-1, width).astype(jnp.float32)
    mixed = jnp.dot(combine, expert_out, precision=lax.Precision.HIGHEST)
    return mixed.astype(jnp.bfloat16)


def solution(mesh):
    in_specs = (
        P(("grp", "ep", "dp"), None),
        P(("grp", "ep", "dp"), None),
        P(("grp", "ep", "dp"), None),
        P(),
        P("ep", None, "dp"),
        P("ep", None, "dp"),
        P("ep", "dp", None),
    )
    out_specs = P(("grp", "ep", "dp"), None)
    return jax.shard_map(body, mesh=mesh, in_specs=in_specs, out_specs=out_specs, check_vma=False)
```

profile of v0, /device:TPU:0, one launch (start us, length us, event | category | flops | bytes accessed | tf_op | source)
XLA Modules:
  0.0 203.7 jit_solution(4430710558745166159)
XLA Ops:
  6.5 0.0 copy-start
  6.5 0.0 all-gather.3.cloned.1.call-start
  6.5 0.8 eq.43
  7.3 0.8 select_reduce_fusion.1
  8.2 0.1 fusion.35
  8.2 0.1 reduce_window_sum.11
  8.3 0.2 select_reduce_fusion
  8.5 0.1 add.17
  8.6 0.1 convert_reduce_fusion
  8.7 0.0 copy-done
  8.7 0.4 convolution_convert_fusion
  9.1 0.4 reshape.37
  9.5 0.4 copy.20
  9.9 24.2 %all_to_all.10 = bf16[4,4,3,7168]{3,1,2,0:T(4,128)(2,1)} all-to-all(bf16[4,4,3,7168]{3,1,2,0:T(4,128)(2,1)S(1)} %copy.20), channel_id=1, replica_groups=mesh['grp'=2,'ep'=4,'dp'=4] {'ep'}, dimensions={0} | all-to-all | bytes 1376256 | tf_op jit(solution)/shard_map/all_to_all | solution.py:41
  34.2 0.0 all-gather.3.cloned.1.call-update
  34.2 0.0 all-reduce.3.cloned.1.call-start
  34.2 25.5 %all-gather.3.cloned.1.call-done = bf16[16,4,3,7168]{3,1,2,0:T(4,128)(2,1)} async-done(((bf16[4,4,3,7168]{3,1,2,0:T(4,128)(2,1)}), bf16[16,4,3,7168]{3,1,2,0:T(4,128)(2,1)}) %all-gather.3.cloned.1.call-update) | async-done | bytes 2752528 | tf_op jit(solution)/shard_map/all_gather | solution.py:43
  59.8 0.0 copy-start.2
  59.8 17.2 %fusion.14 = f32[4,4,4,3,512]{4,1,3,0,2:T(4,128)S(1)} fusion(bf16[4,7168,512]{2,1,0:T(8,128)(2,1)} %param.11, bf16[4,4,4,3,7168]{4,2,3,1,0:T(4,128)(2,1)} %bitcast.55), kind=kOutput, calls=%fused_computation.12 | convolution fusion | flops 1409286144 | bytes 32505856 | tf_op jit(solution)/shard_map/kpjcd,jdf->kpjcf/dot_general | solution.py:26
  77.0 0.0 copy-done.2
  77.0 13.5 %fusion.29 = bf16[4,4,4,3,512]{4,1,3,0,2:T(4,128)(2,1)S(1)} fusion(bf16[4,7168,512]{2,1,0:T(8,128)(2,1)} %param.12, bf16[4,4,4,3,7168]{4,2,3,1,0:T(4,128)(2,1)S(1)} %bitcast.56, f32[4,4,4,3,512]{4,1,3,0,2:T(4,128)S(1)} %fusion.14), kind=kOutput, calls=%fused_computation.15 | convolution fusion | flops 1409875968 | bytes 32702464 | tf_op jit(solution)/shard_map/kpjcd,jdf->kpjcf/dot_general | solution.py:27
  90.6 16.3 %fusion.9 = bf16[4,4,4,3,7168]{4,1,3,0,2:T(4,128)(2,1)} fusion(bf16[4,4,4,3,512]{4,1,3,0,2:T(4,128)(2,1)S(1)} %fusion.29, bf16[4,512,7168]{2,1,0:T(8,128)(2,1)} %param.13), kind=kOutput, calls=%fused_computation.7 | convolution fusion | flops 1410662400 | bytes 32309248 | tf_op jit(solution)/shard_map/kpjcf,jfd->kpjcd/dot_general | solution.py:29
  106.8 0.0 copy-start.4
  106.8 0.0 all-reduce.3.cloned.1.call-update
  106.9 0.0 copy-start.3
  106.9 0.6 copy-done.4
  107.5 0.6 dynamic-slice
  108.1 61.0 %all-reduce.3.cloned.1.call-done = bf16[4,4,4,3,7168]{4,1,3,0,2:T(4,128)(2,1)} async-done(((bf16[4,4,4,3,7168]{4,1,3,0,2:T(4,128)(2,1)}), bf16[4,4,4,3,7168]{4,1,3,0,2:T(4,128)(2,1)}) %all-reduce.3.cloned.1.call-update) | async-done | bytes 2752528
  169.1 2.0 constant_dynamic-slice_fusion
  171.0 0.0 copy-start.1
  171.1 1.2 copy.23
  172.3 4.6 %all-to-all-start.1 = ((bf16[1,4,4,3,7168]{4,2,3,0,1:T(4,128)(2,1)}), bf16[1,4,4,3,7168]{4,2,3,0,1:T(4,128)(2,1)S(1)}, u32[]{:S(2)}, u32[]{:S(2)}) async-start(bf16[1,4,4,3,7168]{4,2,3,0,1:T(4,128)(2,1)} %copy.23), calls=%async_computation.1 | async-start | bytes 1376256 | tf_op jit(solution)/shard_map/all_to_all | solution.py:48
  176.9 0.0 copy-done.3
  176.9 0.2 fusion.34
  177.1 17.7 %all-to-all-done.1 = bf16[1,4,4,3,7168]{4,2,3,0,1:T(4,128)(2,1)S(1)} async-done(((bf16[1,4,4,3,7168]{4,2,3,0,1:T(4,128)(2,1)}), bf16[1,4,4,3,7168]{4,2,3,0,1:T(4,128)(2,1)S(1)}, u32[]{:S(2)}, u32[]{:S(2)}) %all-to-all-start.1) | async-done | bytes 688160 | tf_op jit(solution)/shard_map/all_to_all | solution.py:48
  194.8 0.5 copy.24
  195.3 0.6 reshape.38
  195.9 1.0 convolution_convert_fusion.1
  196.9 0.0 copy-done.1
  (1 shorter events, 0.0 us)
Async XLA Ops:
  6.5 2.1 %copy-start = (bf16[4,7168]{1,0:T(4,128)(2,1)S(1)}, bf16[4,7168]{1,0:T(4,128)(2,1)}, u32[]{:S(2)}) copy-start(bf16[4,7168]{1,0:T(4,128)(2,1)} %param.7) | copy-start | bytes 172036
  6.5 53.2 %all-gather.3.cloned.1.call-start = ((), (), s32[]{:S(2)}) async-start(), calls=%async_computation.2 | async-start | bytes 3440640 | tf_op jit(solution)/shard_map/all_gather | solution.py:43
  34.2 134.9 %all-reduce.3.cloned.1.call-start = ((), (), s32[]{:S(2)}) async-start(), calls=%async_computation.3 | async-start | bytes 5505024
  59.8 17.3 %copy-start.2 = (bf16[16,4,3,7168]{3,1,2,0:T(4,128)(2,1)S(1)}, bf16[16,4,3,7168]{3,1,2,0:T(4,128)(2,1)}, u32[]{:S(2)}) copy-start(bf16[16,4,3,7168]{3,1,2,0:T(4,128)(2,1)} %all-gather.3.cloned.1.call-done) | copy-start | bytes 8257540
  106.8 0.7 copy-start.4
  106.9 70.0 %copy-start.3 = (f32[4,8]{1,0:T(4,128)S(1)}, f32[4,8]{1,0:T(4,128)}, u32[]{:S(2)}) copy-start(f32[4,8]{1,0:T(4,128)} %param.9) | copy-start | bytes 388
  171.0 25.8 %copy-start.1 = (bf16[4,7168]{1,0:T(4,128)(2,1)S(1)}, bf16[4,7168]{1,0:T(4,128)(2,1)}, u32[]{:S(2)}) copy-start(bf16[4,7168]{1,0:T(4,128)(2,1)} %param.7) | copy-start | bytes 172036
  172.3 22.5 %all-to-all-start.1 = ((bf16[1,4,4,3,7168]{4,2,3,0,1:T(4,128)(2,1)}), bf16[1,4,4,3,7168]{4,2,3,0,1:T(4,128)(2,1)S(1)}, u32[]{:S(2)}, u32[]{:S(2)}) async-start(bf16[1,4,4,3,7168]{4,2,3,0,1:T(4,128)(2,1)} %copy.23), calls=%async_computation.1 | async-start | bytes 1376256 | tf_op jit(solution)/shard_map/all_to_all | solution.py:48
Sparse Core Ops, SparseCore 0:
  34.3 25.3 all-gather.2
  107.0 62.0 all-reduce.2
where the time goes:
time: 204 us
  waiting for transfers between devices  104 us (51%)
  matrix products  48.6 us (24%)
  blocking collectives  24.2 us (12%)
  between operations  13.5 us (7%)
  local copies, waits for them, and re-layouts  7.23 us (4%)
  starting transfers between devices  4.64 us (2%)
    unnamed x3, waiting for transfers between devices  61 us
    all_gather x1, waiting for transfers between devices, body(): lax.all_gather(arrived[None], 'dp', axis=0, tiled=True)  25.5 us
    all_to_all x1, blocking collectives, body(): lax.all_to_all(outgoing, 'ep', split_axis=0, concat_axis=0, tiled=True)  24.2 us
    all_to_all x1, waiting for transfers between devices, body(): lax.all_to_all(summed, 'ep', split_axis=1, concat_axis=1, tiled=True)  17.7 us
    dot_general x1, matrix products, expert_rows(): jnp.einsum('kpjcd,jdf->kpjcf', piece, w_gate, preferred_element_type=jnp....  17.2 us
    dot_general x1, matrix products, expert_rows(): jnp.einsum('kpjcf,jfd->kpjcd', hidden, w_down, preferred_element_type=jnp...  16.3 us
    dot_general x1, matrix products, expert_rows(): jnp.einsum('kpjcd,jdf->kpjcf', piece, w_up, preferred_element_type=jnp.fl...  13.5 us
    all_to_all x1, starting transfers between devices, body(): lax.all_to_all(summed, 'ep', split_axis=1, concat_axis=1, tiled=True)  4.6 us
  transfers between devices with their start and end apart: 3, of which 3 were waited for; matrix products, arithmetic and copies ran while one was open for 0% of the time, Pallas kernels for 0%

commit v1 on v0

v1 whole, which is shorter than its diff:
```python
import functools

import jax
import jax.numpy as jnp
from jax import lax
from jax.experimental import pallas as pl
from jax.experimental.pallas import tpu as pltpu
from jax.sharding import PartitionSpec as P

LANES = 128
PACK = 16
SOURCES = 16
HALVES = 2
MESH = pl.DeviceIdType.MESH


def slot_weights(expert_ids, combine_weight, slot_of_expert):
    experts = slot_of_expert.shape[0]
    numbers = jnp.arange(experts, dtype=jnp.int32)
    chosen = expert_ids[:, :, None] == numbers
    picked = jnp.sum(jnp.where(chosen, slot_of_expert, 0), axis=2)
    return jnp.sum(
        jnp.where(picked[:, :, None] == numbers, combine_weight[:, :, None], 0.0), axis=1
    )


def order(rows, transposed):
    side = SOURCES * PACK
    bits = rows.bit_length() - 1
    long = lax.broadcasted_iota(jnp.int32, (side, side), 1 if transposed else 0)
    short = lax.broadcasted_iota(jnp.int32, (side, side), 0 if transposed else 1)
    token = long & (rows - 1)
    device = (long >> bits) & (SOURCES - 1)
    piece = long >> (bits + SOURCES.bit_length() - 1)
    return jnp.where(short == device * PACK + piece * rows + token, 1.0, 0.0).astype(jnp.bfloat16)


def kernel(n, n_dp, rows, x_ref, wg_ref, wu_ref, wd_ref, o_ref,
           xbuf, xs, comb, wg, wu, wd, hid, ybuf, sbuf, rbuf,
           g_sem, u_sem, d_sem, xs_sem, xr_sem, rs_sem, rr_sem):
    slots = wg_ref.shape[0]
    pieces = PACK // rows
    sets = wg.shape[0]
    ring = wd.shape[0]
    span = wg.shape[2]
    half = wd.shape[2]
    part = half // pieces
    block = SOURCES * rows
    ep = lax.axis_index("ep")
    dp = lax.axis_index("dp")
    me = ep * n_dp + dp

    def gate_copies(s, place, c):
        source = (s, pl.ds(c * span, span))
        return (
            pltpu.make_async_copy(wg_ref.at[source], wg.at[place, c], g_sem.at[place, c]),
            pltpu.make_async_copy(wu_ref.at[source], wu.at[place, c], u_sem.at[place, c]),
        )

    def down_copy(i):
        return pltpu.make_async_copy(
            wd_ref.at[i % slots, :, pl.ds((i // slots) * half, half)], wd.at[i % ring], d_sem.at[i % ring]
        )

    def partner(d):
        p = lax.rem(me + d, n)
        return p, {"ep": lax.div(p, n_dp), "dp": lax.rem(p, n_dp)}

    barrier = pltpu.get_barrier_semaphore()

    def greet(d, _):
        pl.semaphore_signal(barrier, inc=1, device_id=partner(d)[1], device_id_type=MESH)
        return 0

    lax.fori_loop(1, n, greet, 0)
    for s in range(sets):
        for c in range(pieces):
            for copy in gate_copies(s, s, c):
                copy.start()
    for i in range(ring):
        down_copy(i).start()
    pl.semaphore_wait(barrier, n - 1)

    def x_copy(d):
        p, where = partner(d)
        return pltpu.make_async_remote_copy(
            src_ref=x_ref, dst_ref=xbuf.at[me], send_sem=xs_sem.at[p], recv_sem=xr_sem.at[me],
            device_id=where, device_id_type=MESH,
        )

    def x_arrival(d):
        p, where = partner(d)
        return pltpu.make_async_remote_copy(
            src_ref=x_ref, dst_ref=xbuf.at[p], send_sem=xs_sem.at[p], recv_sem=xr_sem.at[p],
            device_id=where, device_id_type=MESH,
        )

    def x_send(d, _):
        x_copy(d).start()
        return 0

    lax.fori_loop(1, n, x_send, 0)
    xbuf[me] = x_ref[...]

    def x_wait(d, _):
        x_arrival(d).wait_recv()
        return 0

    lax.fori_loop(1, n, x_wait, 0)

    forward = order(rows, False)

    def unpack(b, _):
        packed = xbuf[pl.ds(b * SOURCES, SOURCES)].reshape(SOURCES * PACK, span + LANES)
        here = pl.ds(pl.multiple_of(b * block, block), block)
        plain = jnp.dot(forward, packed, preferred_element_type=jnp.float32)
        total = plain[:block, span:]
        for c in range(1, pieces):
            total = total + plain[c * block:(c + 1) * block, span:]
        comb[here] = total
        for c in range(pieces):
            xs[c, here] = plain[c * block:(c + 1) * block, :span].astype(jnp.bfloat16)
        return 0

    lax.fori_loop(0, n // SOURCES, unpack, 0)

    def slot_step(s, _):
        place = lax.rem(s, sets)
        gate = upper = None
        for c in range(pieces):
            for copy in gate_copies(s, place, c):
                copy.wait()
            g = jnp.dot(xs[c], wg[place, c], preferred_element_type=jnp.float32)
            u = jnp.dot(xs[c], wu[place, c], preferred_element_type=jnp.float32)
            gate = g if c == 0 else gate + g
            upper = u if c == 0 else upper + u

            @pl.when(s + sets < slots)
            def _():
                for copy in gate_copies(s + sets, place, c):
                    copy.start()

        table = comb[...]
        lane = lax.broadcasted_iota(jnp.int32, table.shape, 1)
        scale = jnp.sum(jnp.where(lane == ep * slots + s, table, 0.0), axis=1, keepdims=True)
        hidden = gate / (1.0 + jnp.exp(-gate)) * upper
        hid[s] = (hidden * scale).astype(jnp.bfloat16)
        return 0

    lax.fori_loop(0, slots, slot_step, 0)

    back = order(rows, True)

    def r_copy(h, d):
        p, where = partner(d)
        return pltpu.make_async_remote_copy(
            src_ref=sbuf.at[h, p], dst_ref=rbuf.at[h, me], send_sem=rs_sem.at[h, p],
            recv_sem=rr_sem.at[h, me], device_id=where, device_id_type=MESH,
        )

    def r_arrival(h, d):
        p, where = partner(d)
        return pltpu.make_async_remote_copy(
            src_ref=sbuf.at[h, p], dst_ref=rbuf.at[h, p], send_sem=rs_sem.at[h, p],
            recv_sem=rr_sem.at[h, p], device_id=where, device_id_type=MESH,
        )

    for h in range(HALVES):
        for s in range(slots):
            down_copy(h * slots + s).wait()
        for c in range(pieces):
            columns = slice(c * part, (c + 1) * part)
            total = None
            for s in range(slots):
                y = jnp.dot(hid[s], wd[(h * slots + s) % ring, :, columns],
                            preferred_element_type=jnp.float32)
                total = y if s == 0 else total + y
            ybuf[:, c] = total.astype(jnp.bfloat16).reshape(n // SOURCES, block, part)
        for s in range(slots):
            later = h * slots + s + ring
            if later < HALVES * slots:
                down_copy(later).start()

        def pack(b, _):
            plain = ybuf[b].reshape(pieces * block, part)
            packed = jnp.dot(back, plain, preferred_element_type=jnp.float32)
            sbuf[h, pl.ds(b * SOURCES, SOURCES)] = packed.astype(jnp.bfloat16).reshape(
                SOURCES, PACK, part)
            return 0

        lax.fori_loop(0, n // SOURCES, pack, 0)

        def r_send(d, _):
            r_copy(h, d).start()
            return 0

        lax.fori_loop(1, n, r_send, 0)
        rbuf[h, me] = sbuf[h, me]

    def x_sent(d, _):
        x_copy(d).wait_send()
        return 0

    lax.fori_loop(1, n, x_sent, 0)
    for h in range(HALVES):
        def r_wait(d, _):
            r_arrival(h, d).wait_recv()
            return 0

        lax.fori_loop(1, n, r_wait, 0)

        def add(i, total):
            return total + rbuf[h, i].astype(jnp.float32)

        total = lax.fori_loop(0, n, add, jnp.zeros((PACK, part), jnp.float32))
        o_ref[h] = total.astype(jnp.bfloat16)

        def r_sent(d, _):
            r_copy(h, d).wait_send()
            return 0

        lax.fori_loop(1, n, r_sent, 0)


def body(tokens, expert_ids, combine_weight, slot_of_expert, w_gate, w_up, w_down):
    n_dp = lax.axis_size("dp")
    n = lax.axis_size("ep") * n_dp
    rows, width = tokens.shape
    slots, _, units = w_gate.shape
    pieces = PACK // rows
    span = width // pieces
    half = width // HALVES
    part = half // pieces
    sets = min(2, slots)
    ring = min(6, HALVES * slots)
    table = slot_weights(expert_ids, combine_weight, slot_of_expert)
    high = lax.reduce_precision(table, 8, 7)
    middle = lax.reduce_precision(table - high, 8, 7)
    low = table - high - middle
    extra = jnp.stack([high, middle, low] + [jnp.zeros_like(low)] * (pieces - 3))
    extra = jnp.pad(extra, ((0, 0), (0, 0), (0, LANES - extra.shape[2])))
    packed = jnp.concatenate([
        jnp.transpose(tokens.reshape(rows, pieces, span), (1, 0, 2)).reshape(PACK, span),
        extra.reshape(PACK, LANES).astype(jnp.bfloat16),
    ], axis=1)
    vmem = pl.BlockSpec(memory_space=pltpu.VMEM)
    hbm = pl.BlockSpec(memory_space=pl.ANY)
    bf16 = jnp.bfloat16
    dma = pltpu.SemaphoreType.DMA
    out = pl.pallas_call(
        functools.partial(kernel, n, n_dp, rows),
        out_shape=jax.ShapeDtypeStruct((HALVES, PACK, part), bf16),
        in_specs=[vmem, hbm, hbm, hbm],
        out_specs=vmem,
        scratch_shapes=[
            pltpu.VMEM((n, PACK, span + LANES), bf16),
            pltpu.VMEM((pieces, n * rows, span), bf16),
            pltpu.VMEM((n * rows, LANES), jnp.float32),
            pltpu.VMEM((sets, pieces, span, units), bf16),
            pltpu.VMEM((sets, pieces, span, units), bf16),
            pltpu.VMEM((ring, units, half), bf16),
            pltpu.VMEM((slots, n * rows, units), bf16),
            pltpu.VMEM((n // SOURCES, pieces, SOURCES * rows, part), bf16),
            pltpu.VMEM((HALVES, n, PACK, part), bf16),
            pltpu.VMEM((HALVES, n, PACK, part), bf16),
            dma((sets, pieces)),
            dma((sets, pieces)),
            dma((ring,)),
            dma((n,)),
            dma((n,)),
            dma((HALVES, n)),
            dma((HALVES, n)),
        ],
        compiler_params=pltpu.CompilerParams(
            collective_id=0, has_side_effects=True, vmem_limit_bytes=60 * 2**20
        ),
        cost_estimate=pl.CostEstimate(
            flops=6 * n * rows * slots * width * units,
            bytes_accessed=6 * slots * width * units,
            transcendentals=n * rows * slots * units,
        ),
    )(packed, w_gate, w_up, w_down)
    out = out.reshape(HALVES, pieces, rows, part)
    return jnp.transpose(out, (2, 0, 1, 3)).reshape(rows, width)


def solution(mesh):
    in_specs = (
        P(("grp", "ep", "dp"), None),
        P(("grp", "ep", "dp"), None),
        P(("grp", "ep", "dp"), None),
        P(),
        P("ep", None, "dp"),
        P("ep", None, "dp"),
        P("ep", "dp", None),
    )
    out_specs = P(("grp", "ep", "dp"), None)
    return jax.shard_map(body, mesh=mesh, in_specs=in_specs, out_specs=out_specs, check_vma=False)
```

time: 204 us -> 67.4 us (0.33)
  the two profiles are of different devices: /device:TPU:0 before, /device:TPU:27 now
where the time goes in v1:
time: 67.4 us; the launch traced here: 67.1 us
  Pallas kernels  62.3 us (92%)
  other arithmetic  2.39 us (4%)
  local copies, waits for them, and re-layouts  2.38 us (4%)
    pallas_call x1, Pallas kernels, body(): pl.pallas_call(functools.partial(kernel, n, n_dp, rows), out_shape=jax.Sh...  62.3 us
    reshape x1, local copies, waits for them, and re-layouts, body(): out = out.reshape(HALVES, pieces, rows, part)  1.46 us

profile of v1, /device:TPU:27, one launch (start us, length us, event | category | flops | bytes accessed | tf_op | source)
XLA Modules:
  0.0 67.1 jit_solution(16941012548113018447)
XLA Ops:
  0.0 0.1 pad.11.clone
  0.1 0.9 %select_reduce_fusion.1 = s32[4,8]{1,0:T(4,128)S(1)} fusion(s32[16]{0:T(128)} %param.10, s32[4,8]{1,0:T(4,128)} %param.8), kind=kLoop, calls=%fused_computation.3 | loop fusion | flops 1504 | bytes 320 | tf_op jit(solution)/shard_map/reduce_sum | solution.py:21
  1.0 0.8 %select_reduce_fusion = f32[4,16]{1,0:T(4,128)S(1)} fusion(f32[4,8]{1,0:T(4,128)} %param.9, s32[4,8]{1,0:T(4,128)S(1)} %select_reduce_fusion.1), kind=kLoop, calls=%fused_computation.1 | loop fusion | flops 1472 | bytes 512 | tf_op jit(solution)/shard_map/reduce_sum | solution.py:22
  1.8 0.1 maximum_maximum_fusion
  1.9 0.8 %reshape.42 = bf16[16,1792]{1,0:T(8,128)(2,1)S(1)} reshape(bf16[4,4,1792]{2,1,0:T(4,128)(2,1)} %bitcast.15) | data formatting | bytes 114688 | tf_op jit(solution)/shard_map/reshape | solution.py:243
  2.7 0.6 pad_maximum_fusion.x_ref
  3.3 62.3 %shard_map.73 = bf16[2,16,896]{2,1,0:T(8,128)(2,1)} custom-call(bf16[16,1920]{1,0:T(8,128)(2,1)} %pad_maximum_fusion.x_ref, bf16[4,7168,512]{2,1,0:T(8,128)(2,1)} %wg_ref.1, bf16[4,7168,512]{2,1,0:T(8,128)(2,1)} %wu_ref.1, bf16[4,512,7168]{2,1,0:T(8,128)(2,1)} %wd_ref.1), custom_call_target="tpu_custom_call" | custom-call | flops 5637144576 | bytes 88080384 | tf_op jit(solution)/shard_map/pallas_call | solution.py:250
  65.6 1.5 %reshape.43 = bf16[2,4,4,896]{3,2,1,0:T(4,128)(2,1)} reshape(bf16[2,16,896]{2,1,0:T(8,128)(2,1)} %shard_map.73) | data formatting | bytes 114688 | tf_op jit(solution)/shard_map/reshape | solution.py:283
  (2 shorter events, 0.0 us)

commit v2 on v1

v2 whole, which is shorter than its diff:
```python
import functools

import jax
import jax.numpy as jnp
from jax import lax
from jax.experimental import pallas as pl
from jax.experimental.pallas import tpu as pltpu
from jax.sharding import PartitionSpec as P

LANES = 128
PACK = 16
SOURCES = 16
HALVES = 2
MESH = pl.DeviceIdType.MESH


def slot_weights(ids, weights, slot_ref):
    shape = (ids.shape[0], LANES)
    lane = lax.broadcasted_iota(jnp.int32, shape, 1)
    by_expert = jnp.zeros(shape, jnp.float32)
    for k in range(ids.shape[1]):
        by_expert += jnp.where(lane == ids[:, k:k + 1], weights[:, k:k + 1], 0.0)
    by_slot = jnp.zeros(shape, jnp.float32)
    for e in range(slot_ref.shape[0]):
        by_slot += jnp.where(lane == slot_ref[e], by_expert[:, e:e + 1], 0.0)
    return by_slot


def order(rows, transposed):
    side = SOURCES * PACK
    bits = rows.bit_length() - 1
    long = lax.broadcasted_iota(jnp.int32, (side, side), 1 if transposed else 0)
    short = lax.broadcasted_iota(jnp.int32, (side, side), 0 if transposed else 1)
    token = long & (rows - 1)
    device = (long >> bits) & (SOURCES - 1)
    piece = long >> (bits + SOURCES.bit_length() - 1)
    if transposed:
        device = (device & 1) * (SOURCES // 2) + (device >> 1)
    return jnp.where(short == device * PACK + piece * rows + token, 1.0, 0.0).astype(jnp.bfloat16)


def kernel(n, n_dp, rows, t_ref, id_ref, cw_ref, so_ref, wg_ref, wu_ref, wd_ref, o_ref,
           xp, xbuf, xs, comb, wg, wu, wd, hid, ybuf, sbuf, pbuf, tbuf, rbuf,
           g_sem, u_sem, d_sem, xs_sem, xr_sem, fs_sem, ps_sem, pr_sem, rs_sem, rr_sem):
    slots = wg_ref.shape[0]
    pieces = PACK // rows
    sets = wg.shape[0]
    ring = wd.shape[0]
    span = wg.shape[2]
    half = wd.shape[2]
    part = half // pieces
    block = SOURCES * rows
    ep = lax.axis_index("ep")
    dp = lax.axis_index("dp")
    me = ep * n_dp + dp
    chips = n // 2
    chip, core = lax.div(me, 2), lax.rem(me, 2)
    other = 1 - core

    def gate_copies(s, place, c):
        source = (s, pl.ds(c * span, span))
        return (
            pltpu.make_async_copy(wg_ref.at[source], wg.at[place, c], g_sem.at[place, c]),
            pltpu.make_async_copy(wu_ref.at[source], wu.at[place, c], u_sem.at[place, c]),
        )

    def down_copy(i):
        return pltpu.make_async_copy(
            wd_ref.at[i % slots, :, pl.ds((i // slots) * half, half)], wd.at[i % ring], d_sem.at[i % ring]
        )

    def place_of(p):
        return {"ep": lax.div(p, n_dp), "dp": lax.rem(p, n_dp)}

    sibling = place_of(2 * chip + other)

    def ahead(d):
        return lax.rem(chip + d, chips)

    def behind(d):
        return lax.rem(chip + chips - d, chips)

    barrier = pltpu.get_barrier_semaphore()

    def greet(d, _):
        pl.semaphore_signal(
            barrier, inc=1, device_id=place_of(2 * ahead(d) + core), device_id_type=MESH)
        return 0

    pl.semaphore_signal(barrier, inc=1, device_id=sibling, device_id_type=MESH)
    lax.fori_loop(1, chips, greet, 0)
    for s in range(sets):
        for c in range(pieces):
            for copy in gate_copies(s, s, c):
                copy.start()
    for i in range(ring):
        down_copy(i).start()
    table = slot_weights(id_ref[...], cw_ref[...], so_ref)
    high = table.astype(jnp.bfloat16).astype(jnp.float32)
    middle = (table - high).astype(jnp.bfloat16).astype(jnp.float32)
    terms = [high, middle, table - high - middle] + [jnp.zeros_like(table)] * (pieces - 3)
    xp[:, :span] = jnp.concatenate(
        [t_ref[:, c * span:(c + 1) * span].astype(jnp.float32) for c in range(pieces)], axis=0
    ).astype(jnp.bfloat16)
    xp[:, span:] = jnp.concatenate(terms, axis=0).astype(jnp.bfloat16)
    pl.semaphore_wait(barrier, chips)

    def x_copy(source, target, to_chip, to_core, landed, sent):
        return pltpu.make_async_remote_copy(
            src_ref=source, dst_ref=xbuf.at[target], send_sem=sent, recv_sem=xr_sem.at[landed],
            device_id=place_of(2 * to_chip + to_core), device_id_type=MESH,
        )

    def x_send(d, _):
        x_copy(xp, me, ahead(d), core, me, xs_sem.at[ahead(d)]).start()
        return 0

    def x_pass(d, _):
        p = 2 * behind(d) + core
        x_copy(xp, p, behind(d), core, p, xs_sem.at[behind(d)]).wait_recv()
        x_copy(xbuf.at[p], p, chip, other, p, fs_sem.at[behind(d)]).start()
        return 0

    def x_wait(d, _):
        p = 2 * behind(d) + other
        x_copy(xp, p, chip, other, p, fs_sem.at[behind(d)]).wait_recv()
        return 0

    lax.fori_loop(1, chips, x_send, 0)
    x_copy(xp, me, chip, other, me, fs_sem.at[chip]).start()
    xbuf[me] = xp[...]
    lax.fori_loop(1, chips, x_pass, 0)
    lax.fori_loop(0, chips, x_wait, 0)

    forward = order(rows, False)

    def unpack(b, _):
        packed = xbuf[pl.ds(b * SOURCES, SOURCES)].reshape(SOURCES * PACK, span + LANES)
        here = pl.ds(pl.multiple_of(b * block, block), block)
        plain = jnp.dot(forward, packed, preferred_element_type=jnp.float32)
        total = plain[:block, span:]
        for c in range(1, pieces):
            total = total + plain[c * block:(c + 1) * block, span:]
        comb[here] = total
        for c in range(pieces):
            xs[c, here] = plain[c * block:(c + 1) * block, :span].astype(jnp.bfloat16)
        return 0

    lax.fori_loop(0, n // SOURCES, unpack, 0)

    def slot_step(s, _):
        place = lax.rem(s, sets)
        gate = upper = None
        for c in range(pieces):
            for copy in gate_copies(s, place, c):
                copy.wait()
            g = jnp.dot(xs[c], wg[place, c], preferred_element_type=jnp.float32)
            u = jnp.dot(xs[c], wu[place, c], preferred_element_type=jnp.float32)
            gate = g if c == 0 else gate + g
            upper = u if c == 0 else upper + u

            @pl.when(s + sets < slots)
            def _():
                for copy in gate_copies(s + sets, place, c):
                    copy.start()

        table = comb[...]
        lane = lax.broadcasted_iota(jnp.int32, table.shape, 1)
        scale = jnp.sum(jnp.where(lane == ep * slots + s, table, 0.0), axis=1, keepdims=True)
        hidden = gate / (1.0 + jnp.exp(-gate)) * upper
        hid[s] = (hidden * scale).astype(jnp.bfloat16)
        return 0

    lax.fori_loop(0, slots, slot_step, 0)

    back = order(rows, True)

    def pair_copy(h):
        return pltpu.make_async_remote_copy(
            src_ref=sbuf.at[h, other], dst_ref=pbuf.at[h], send_sem=ps_sem.at[h],
            recv_sem=pr_sem.at[h], device_id=sibling, device_id_type=MESH,
        )

    def r_copy(h, to, landed):
        return pltpu.make_async_remote_copy(
            src_ref=tbuf.at[h, to], dst_ref=rbuf.at[h, landed], send_sem=rs_sem.at[h, to],
            recv_sem=rr_sem.at[h, landed], device_id=place_of(2 * to + core), device_id_type=MESH,
        )

    def reduce_pair(h):
        pair_copy(h).wait()

        def r_send(d, _):
            to = ahead(d)
            both = sbuf[h, core, to].astype(jnp.float32) + pbuf[h, to].astype(jnp.float32)
            tbuf[h, to] = both.astype(jnp.bfloat16)
            r_copy(h, to, chip).start()
            return 0

        lax.fori_loop(1, chips, r_send, 0)

    for h in range(HALVES):
        for s in range(slots):
            down_copy(h * slots + s).wait()
        for c in range(pieces):
            columns = slice(c * part, (c + 1) * part)
            total = None
            for s in range(slots):
                y = jnp.dot(hid[s], wd[(h * slots + s) % ring, :, columns],
                            preferred_element_type=jnp.float32)
                total = y if s == 0 else total + y
            if h > 0 and c == 0:
                reduce_pair(h - 1)
            ybuf[:, c] = total.astype(jnp.bfloat16).reshape(n // SOURCES, block, part)
        for s in range(slots):
            later = h * slots + s + ring
            if later < HALVES * slots:
                down_copy(later).start()

        def pack(b, _):
            plain = ybuf[b].reshape(pieces * block, part)
            packed = jnp.dot(back, plain, preferred_element_type=jnp.float32)
            packed = packed.astype(jnp.bfloat16).reshape(2, SOURCES // 2, PACK, part)
            sbuf[h, :, pl.ds(b * (SOURCES // 2), SOURCES // 2)] = packed
            return 0

        lax.fori_loop(0, n // SOURCES, pack, 0)
        pair_copy(h).start()
    reduce_pair(HALVES - 1)

    def x_sent(d, _):
        x_copy(xp, me, ahead(d), core, me, xs_sem.at[ahead(d)]).wait_send()
        return 0

    def x_passed(d, _):
        x_copy(xp, me, chip, other, me, fs_sem.at[behind(d)]).wait_send()
        return 0

    lax.fori_loop(1, chips, x_sent, 0)
    lax.fori_loop(0, chips, x_passed, 0)
    for h in range(HALVES):
        total = sbuf[h, core, chip].astype(jnp.float32) + pbuf[h, chip].astype(jnp.float32)

        def add(d, total):
            r_copy(h, behind(d), behind(d)).wait_recv()
            return total + rbuf[h, behind(d)].astype(jnp.float32)

        total = lax.fori_loop(1, chips, add, total)
        for c in range(pieces):
            o_ref[:, h * half + c * part:h * half + (c + 1) * part] = (
                total[c * rows:(c + 1) * rows].astype(jnp.bfloat16))

        def r_sent(d, _):
            r_copy(h, ahead(d), chip).wait_send()
            return 0

        lax.fori_loop(1, chips, r_sent, 0)


def body(tokens, expert_ids, combine_weight, slot_of_expert, w_gate, w_up, w_down):
    n_dp = lax.axis_size("dp")
    n = lax.axis_size("ep") * n_dp
    rows, width = tokens.shape
    slots, _, units = w_gate.shape
    pieces = PACK // rows
    span = width // pieces
    half = width // HALVES
    part = half // pieces
    sets = min(2, slots)
    ring = min(6, HALVES * slots)
    vmem = pl.BlockSpec(memory_space=pltpu.VMEM)
    hbm = pl.BlockSpec(memory_space=pl.ANY)
    bf16 = jnp.bfloat16
    dma = pltpu.SemaphoreType.DMA
    return pl.pallas_call(
        functools.partial(kernel, n, n_dp, rows),
        out_shape=jax.ShapeDtypeStruct((rows, width), bf16),
        in_specs=[vmem, vmem, vmem, pl.BlockSpec(memory_space=pltpu.SMEM), hbm, hbm, hbm],
        out_specs=vmem,
        scratch_shapes=[
            pltpu.VMEM((PACK, span + LANES), bf16),
            pltpu.VMEM((n, PACK, span + LANES), bf16),
            pltpu.VMEM((pieces, n * rows, span), bf16),
            pltpu.VMEM((n * rows, LANES), jnp.float32),
            pltpu.VMEM((sets, pieces, span, units), bf16),
            pltpu.VMEM((sets, pieces, span, units), bf16),
            pltpu.VMEM((ring, units, half), bf16),
            pltpu.VMEM((slots, n * rows, units), bf16),
            pltpu.VMEM((n // SOURCES, pieces, SOURCES * rows, part), bf16),
            pltpu.VMEM((HALVES, 2, n // 2, PACK, part), bf16),
            pltpu.VMEM((HALVES, n // 2, PACK, part), bf16),
            pltpu.VMEM((HALVES, n // 2, PACK, part), bf16),
            pltpu.VMEM((HALVES, n // 2, PACK, part), bf16),
            dma((sets, pieces)),
            dma((sets, pieces)),
            dma((ring,)),
            dma((n // 2,)),
            dma((n,)),
            dma((n // 2,)),
            dma((HALVES,)),
            dma((HALVES,)),
            dma((HALVES, n // 2)),
            dma((HALVES, n // 2)),
        ],
        compiler_params=pltpu.CompilerParams(
            collective_id=0, has_side_effects=True, vmem_limit_bytes=60 * 2**20
        ),
        cost_estimate=pl.CostEstimate(
            flops=6 * n * rows * slots * width * units,
            bytes_accessed=6 * slots * width * units,
            transcendentals=n * rows * slots * units,
        ),
    )(tokens, expert_ids, combine_weight, slot_of_expert, w_gate, w_up, w_down)


def solution(mesh):
    in_specs = (
        P(("grp", "ep", "dp"), None),
        P(("grp", "ep", "dp"), None),
        P(("grp", "ep", "dp"), None),
        P(),
        P("ep", None, "dp"),
        P("ep", None, "dp"),
        P("ep", "dp", None),
    )
    out_specs = P(("grp", "ep", "dp"), None)
    return jax.shard_map(body, mesh=mesh, in_specs=in_specs, out_specs=out_specs, check_vma=False)
```

time: 67.4 us -> 50.4 us (0.75)
  the two profiles are of different devices: /device:TPU:27 before, /device:TPU:0 now
where the time goes in v2:
time: 50.4 us; the launch traced here: 50.2 us
  Pallas kernels  48.7 us (97%)
  local copies, waits for them, and re-layouts  1.46 us (3%)
    pallas_call x1, Pallas kernels, body(): pl.pallas_call(functools.partial(kernel, n, n_dp, rows), out_shape=jax.Sh...  48.7 us
    unnamed x1, local copies, waits for them, and re-layouts  1.46 us

profile of v2, /device:TPU:0, one launch (start us, length us, event | category | flops | bytes accessed | tf_op | source)
XLA Modules:
  0.0 50.2 jit_solution(4754900644879650701)
XLA Ops:
  0.0 48.7 %shard_map.73 = bf16[4,7168]{1,0:T(4,128)(2,1)} custom-call(bf16[4,7168]{1,0:T(4,128)(2,1)} %t_ref.1, s32[4,8]{1,0:T(4,128)} %id_ref.1, f32[4,8]{1,0:T(4,128)} %cw_ref.1, s32[16]{0:T(128)} %so_ref.1, bf16[4,7168,512]{2,1,0:T(8,128)(2,1)} %wg_ref.1, bf16[4,7168,512]{2,1,0:T(8,128)(2,1)} %wu_ref.1, bf16[4,512,7168]{2,1,0:T(8,128)(2,1)} %wd_ref.1), custom_call_target="tpu_custom_call" | custom-call | flops 5637144576 | bytes 88080384 | tf_op jit(solution)/shard_map/pallas_call | solution.py:275
  48.7 1.5 %copy.9 = bf16[4,7168]{1,0:T(4,128)(2,1)} copy(bf16[4,7168]{1,0:T(4,128)(2,1)} %shard_map.73) | data formatting | bytes 114688

commit v3 on v2

--- a/solution.py
+++ b/solution.py
@@ -40,13 +40,13 @@
 
 
 def kernel(n, n_dp, rows, t_ref, id_ref, cw_ref, so_ref, wg_ref, wu_ref, wd_ref, o_ref,
-           xp, xbuf, xs, comb, wg, wu, wd, hid, ybuf, sbuf, pbuf, tbuf, rbuf,
+           xp0, xp1, xbuf0, xbuf1, xs, comb, gacc, uacc, wg, wu, wd, hid, ybuf, sbuf, pbuf, tbuf, rbuf,
            g_sem, u_sem, d_sem, xs_sem, xr_sem, fs_sem, ps_sem, pr_sem, rs_sem, rr_sem):
     slots = wg_ref.shape[0]
     pieces = PACK // rows
-    sets = wg.shape[0]
+    depth = wg.shape[0]
+    xp, xbuf = (xp0, xp1), (xbuf0, xbuf1)
     ring = wd.shape[0]
-    span = wg.shape[2]
     half = wd.shape[2]
     part = half // pieces
     block = SOURCES * rows
@@ -57,11 +57,12 @@
     chip, core = lax.div(me, 2), lax.rem(me, 2)
     other = 1 - core
 
-    def gate_copies(s, place, c):
-        source = (s, pl.ds(c * span, span))
+    def gate_copies(step):
+        place = lax.rem(step, depth)
+        source = (lax.rem(step, slots), pl.ds(pl.multiple_of(lax.div(step, slots) * half, half), half))
         return (
-            pltpu.make_async_copy(wg_ref.at[source], wg.at[place, c], g_sem.at[place, c]),
-            pltpu.make_async_copy(wu_ref.at[source], wu.at[place, c], u_sem.at[place, c]),
+            pltpu.make_async_copy(wg_ref.at[source], wg.at[place], g_sem.at[place]),
+            pltpu.make_async_copy(wu_ref.at[source], wu.at[place], u_sem.at[place]),
         )
 
     def down_copy(i):
@@ -89,81 +90,96 @@
 
     pl.semaphore_signal(barrier, inc=1, device_id=sibling, device_id_type=MESH)
     lax.fori_loop(1, chips, greet, 0)
-    for s in range(sets):
-        for c in range(pieces):
-            for copy in gate_copies(s, s, c):
-                copy.start()
+    for step in range(depth):
+        for copy in gate_copies(jnp.int32(step)):
+            copy.start()
     for i in range(ring):
         down_copy(i).start()
     table = slot_weights(id_ref[...], cw_ref[...], so_ref)
     high = table.astype(jnp.bfloat16).astype(jnp.float32)
     middle = (table - high).astype(jnp.bfloat16).astype(jnp.float32)
     terms = [high, middle, table - high - middle] + [jnp.zeros_like(table)] * (pieces - 3)
-    xp[:, :span] = jnp.concatenate(
-        [t_ref[:, c * span:(c + 1) * span].astype(jnp.float32) for c in range(pieces)], axis=0
-    ).astype(jnp.bfloat16)
-    xp[:, span:] = jnp.concatenate(terms, axis=0).astype(jnp.bfloat16)
+    for h in range(HALVES):
+        xp[h][:, :part] = jnp.concatenate(
+            [t_ref[:, h * half + c * part:h * half + (c + 1) * part].astype(jnp.float32)
+             for c in range(pieces)], axis=0).astype(jnp.bfloat16)
+    xp0[:, part:] = jnp.concatenate(terms, axis=0).astype(jnp.bfloat16)
     pl.semaphore_wait(barrier, chips)
 
-    def x_copy(source, target, to_chip, to_core, landed, sent):
+    def across(h, to, landed):
         return pltpu.make_async_remote_copy(
-            src_ref=source, dst_ref=xbuf.at[target], send_sem=sent, recv_sem=xr_sem.at[landed],
-            device_id=place_of(2 * to_chip + to_core), device_id_type=MESH,
-        )
-
-    def x_send(d, _):
-        x_copy(xp, me, ahead(d), core, me, xs_sem.at[ahead(d)]).start()
-        return 0
-
-    def x_pass(d, _):
-        p = 2 * behind(d) + core
-        x_copy(xp, p, behind(d), core, p, xs_sem.at[behind(d)]).wait_recv()
-        x_copy(xbuf.at[p], p, chip, other, p, fs_sem.at[behind(d)]).start()
-        return 0
-
-    def x_wait(d, _):
-        p = 2 * behind(d) + other
-        x_copy(xp, p, chip, other, p, fs_sem.at[behind(d)]).wait_recv()
-        return 0
-
-    lax.fori_loop(1, chips, x_send, 0)
-    x_copy(xp, me, chip, other, me, fs_sem.at[chip]).start()
-    xbuf[me] = xp[...]
-    lax.fori_loop(1, chips, x_pass, 0)
-    lax.fori_loop(0, chips, x_wait, 0)
+            src_ref=xp[h], dst_ref=xbuf[h].at[landed], send_sem=xs_sem.at[h, to],
+            recv_sem=xr_sem.at[h, landed], device_id=place_of(2 * to + core), device_id_type=MESH,
+        )
+
+    def within(h, source, landed):
+        return pltpu.make_async_remote_copy(
+            src_ref=source, dst_ref=xbuf[h].at[landed], send_sem=fs_sem.at[h, lax.div(landed, 2)],
+            recv_sem=xr_sem.at[h, landed], device_id=sibling, device_id_type=MESH,
+        )
+
+    for h in range(HALVES):
+        def x_send(d, _):
+            across(h, ahead(d), me).start()
+            return 0
+
+        lax.fori_loop(1, chips, x_send, 0)
+        within(h, xp[h], me).start()
+        xbuf[h][me] = xp[h][...]
+
+    def pass_on(h):
+        def x_pass(d, _):
+            p = 2 * behind(d) + core
+            across(h, behind(d), p).wait_recv()
+            within(h, xbuf[h].at[p], p).start()
+            return 0
+
+        lax.fori_loop(1, chips, x_pass, 0)
 
     forward = order(rows, False)
 
-    def unpack(b, _):
-        packed = xbuf[pl.ds(b * SOURCES, SOURCES)].reshape(SOURCES * PACK, span + LANES)
-        here = pl.ds(pl.multiple_of(b * block, block), block)
-        plain = jnp.dot(forward, packed, preferred_element_type=jnp.float32)
-        total = plain[:block, span:]
-        for c in range(1, pieces):
-            total = total + plain[c * block:(c + 1) * block, span:]
-        comb[here] = total
-        for c in range(pieces):
-            xs[c, here] = plain[c * block:(c + 1) * block, :span].astype(jnp.bfloat16)
-        return 0
-
-    lax.fori_loop(0, n // SOURCES, unpack, 0)
-
-    def slot_step(s, _):
-        place = lax.rem(s, sets)
-        gate = upper = None
-        for c in range(pieces):
-            for copy in gate_copies(s, place, c):
-                copy.wait()
-            g = jnp.dot(xs[c], wg[place, c], preferred_element_type=jnp.float32)
-            u = jnp.dot(xs[c], wu[place, c], preferred_element_type=jnp.float32)
-            gate = g if c == 0 else gate + g
-            upper = u if c == 0 else upper + u
-
-            @pl.when(s + sets < slots)
-            def _():
-                for copy in gate_copies(s + sets, place, c):
-                    copy.start()
-
+    def gather(h):
+        def x_wait(d, _):
+            within(h, xp[h], 2 * behind(d) + other).wait_recv()
+            return 0
+
+        lax.fori_loop(0, chips, x_wait, 0)
+
+        def unpack(b, _):
+            packed = xbuf[h][pl.ds(b * SOURCES, SOURCES)].reshape(SOURCES * PACK, xbuf[h].shape[2])
+            here = pl.ds(pl.multiple_of(b * block, block), block)
+            plain = jnp.dot(forward, packed, preferred_element_type=jnp.float32)
+            if h == 0:
+                total = plain[:block, part:]
+                for c in range(1, pieces):
+                    total = total + plain[c * block:(c + 1) * block, part:]
+                comb[here] = total
+            for c in range(pieces):
+                xs[h, here, c * part:(c + 1) * part] = (
+                    plain[c * block:(c + 1) * block, :part].astype(jnp.bfloat16))
+            return 0
+
+        lax.fori_loop(0, n // SOURCES, unpack, 0)
+
+    def slot_step(h, s):
+        step = h * slots + s
+        place = lax.rem(step, depth)
+        for copy in gate_copies(step):
+            copy.wait()
+        gate = jnp.dot(xs[h], wg[place], preferred_element_type=jnp.float32)
+        upper = jnp.dot(xs[h], wu[place], preferred_element_type=jnp.float32)
+
+        @pl.when(step + depth < HALVES * slots)
+        def _():
+            for copy in gate_copies(step + depth):
+                copy.start()
+
+        if h == 0:
+            gacc[s] = gate
+            uacc[s] = upper
+            return 0
+        gate = gate + gacc[s]
+        upper = upper + uacc[s]
         table = comb[...]
         lane = lax.broadcasted_iota(jnp.int32, table.shape, 1)
         scale = jnp.sum(jnp.where(lane == ep * slots + s, table, 0.0), axis=1, keepdims=True)
@@ -171,7 +187,14 @@
         hid[s] = (hidden * scale).astype(jnp.bfloat16)
         return 0
 
-    lax.fori_loop(0, slots, slot_step, 0)
+    middle_slot = slots // 2
+    pass_on(0)
+    gather(0)
+    lax.fori_loop(0, middle_slot, lambda s, _: slot_step(0, s), 0)
+    pass_on(1)
+    lax.fori_loop(middle_slot, slots, lambda s, _: slot_step(0, s), 0)
+    gather(1)
+    lax.fori_loop(0, slots, lambda s, _: slot_step(1, s), 0)
 
     back = order(rows, True)
 
@@ -200,22 +223,21 @@
         lax.fori_loop(1, chips, r_send, 0)
 
     for h in range(HALVES):
-        for s in range(slots):
-            down_copy(h * slots + s).wait()
         for c in range(pieces):
             columns = slice(c * part, (c + 1) * part)
             total = None
             for s in range(slots):
+                if c == 0:
+                    down_copy(h * slots + s).wait()
                 y = jnp.dot(hid[s], wd[(h * slots + s) % ring, :, columns],
                             preferred_element_type=jnp.float32)
                 total = y if s == 0 else total + y
+                later = h * slots + s + ring
+                if c == pieces - 1 and later < HALVES * slots:
+                    down_copy(later).start()
             if h > 0 and c == 0:
                 reduce_pair(h - 1)
             ybuf[:, c] = total.astype(jnp.bfloat16).reshape(n // SOURCES, block, part)
-        for s in range(slots):
-            later = h * slots + s + ring
-            if later < HALVES * slots:
-                down_copy(later).start()
 
         def pack(b, _):
             plain = ybuf[b].reshape(pieces * block, part)
@@ -228,16 +250,17 @@
         pair_copy(h).start()
     reduce_pair(HALVES - 1)
 
-    def x_sent(d, _):
-        x_copy(xp, me, ahead(d), core, me, xs_sem.at[ahead(d)]).wait_send()
-        return 0
-
-    def x_passed(d, _):
-        x_copy(xp, me, chip, other, me, fs_sem.at[behind(d)]).wait_send()
-        return 0
-
-    lax.fori_loop(1, chips, x_sent, 0)
-    lax.fori_loop(0, chips, x_passed, 0)
+    for h in range(HALVES):
+        def x_sent(d, _):
+            across(h, ahead(d), me).wait_send()
+            return 0
+
+        def x_passed(d, _):
+            within(h, xp[h], 2 * behind(d) + core).wait_send()
+            return 0
+
+        lax.fori_loop(1, chips, x_sent, 0)
+        lax.fori_loop(0, chips, x_passed, 0)
     for h in range(HALVES):
         total = sbuf[h, core, chip].astype(jnp.float32) + pbuf[h, chip].astype(jnp.float32)
 
@@ -263,11 +286,10 @@
     rows, width = tokens.shape
     slots, _, units = w_gate.shape
     pieces = PACK // rows
-    span = width // pieces
     half = width // HALVES
     part = half // pieces
-    sets = min(2, slots)
-    ring = min(6, HALVES * slots)
+    depth = min(4, HALVES * slots)
+    ring = min(5, HALVES * slots)
     vmem = pl.BlockSpec(memory_space=pltpu.VMEM)
     hbm = pl.BlockSpec(memory_space=pl.ANY)
     bf16 = jnp.bfloat16
@@ -278,12 +300,16 @@
         in_specs=[vmem, vmem, vmem, pl.BlockSpec(memory_space=pltpu.SMEM), hbm, hbm, hbm],
         out_specs=vmem,
         scratch_shapes=[
-            pltpu.VMEM((PACK, span + LANES), bf16),
-            pltpu.VMEM((n, PACK, span + LANES), bf16),
-            pltpu.VMEM((pieces, n * rows, span), bf16),
+            pltpu.VMEM((PACK, part + LANES), bf16),
+            pltpu.VMEM((PACK, part), bf16),
+            pltpu.VMEM((n, PACK, part + LANES), bf16),
+            pltpu.VMEM((n, PACK, part), bf16),
+            pltpu.VMEM((HALVES, n * rows, half), bf16),
             pltpu.VMEM((n * rows, LANES), jnp.float32),
-            pltpu.VMEM((sets, pieces, span, units), bf16),
-            pltpu.VMEM((sets, pieces, span, units), bf16),
+            pltpu.VMEM((slots, n * rows, units), jnp.float32),
+            pltpu.VMEM((slots, n * rows, units), jnp.float32),
+            pltpu.VMEM((depth, half, units), bf16),
+            pltpu.VMEM((depth, half, units), bf16),
             pltpu.VMEM((ring, units, half), bf16),
             pltpu.VMEM((slots, n * rows, units), bf16),
             pltpu.VMEM((n // SOURCES, pieces, SOURCES * rows, part), bf16),
@@ -291,12 +317,12 @@
             pltpu.VMEM((HALVES, n // 2, PACK, part), bf16),
             pltpu.VMEM((HALVES, n // 2, PACK, part), bf16),
             pltpu.VMEM((HALVES, n // 2, PACK, part), bf16),
-            dma((sets, pieces)),
-            dma((sets, pieces)),
+            dma((depth,)),
+            dma((depth,)),
             dma((ring,)),
-            dma((n // 2,)),
-            dma((n,)),
-            dma((n // 2,)),
+            dma((HALVES, n // 2)),
+            dma((HALVES, n)),
+            dma((HALVES, n // 2)),
             dma((HALVES,)),
             dma((HALVES,)),
             dma((HALVES, n // 2)),

time: 50.4 us -> 49.5 us (0.982)
  Pallas kernels: 48.7 us -> 47.8 us
    pallas_call x1, Pallas kernels: 48.7 us -> 47.8 us  [body(): pl.pallas_call(functools.partial(kernel, n, n_dp, rows), out_shape=jax.Sh...]
where the time goes in v3:
time: 49.5 us; the launch traced here: 49.3 us
  Pallas kernels  47.8 us (97%)
  local copies, waits for them, and re-layouts  1.46 us (3%)
    pallas_call x1, Pallas kernels, body(): pl.pallas_call(functools.partial(kernel, n, n_dp, rows), out_shape=jax.Sh...  47.8 us
    unnamed x1, local copies, waits for them, and re-layouts  1.46 us

profile of v3, /device:TPU:0, one launch (start us, length us, event | category | flops | bytes accessed | tf_op | source)
XLA Modules:
  0.0 49.3 jit_solution(12665878794827655118)
XLA Ops:
  0.0 47.8 %shard_map.73 = bf16[4,7168]{1,0:T(4,128)(2,1)} custom-call(bf16[4,7168]{1,0:T(4,128)(2,1)} %t_ref.1, s32[4,8]{1,0:T(4,128)} %id_ref.1, f32[4,8]{1,0:T(4,128)} %cw_ref.1, s32[16]{0:T(128)} %so_ref.1, bf16[4,7168,512]{2,1,0:T(8,128)(2,1)} %wg_ref.1, bf16[4,7168,512]{2,1,0:T(8,128)(2,1)} %wu_ref.1, bf16[4,512,7168]{2,1,0:T(8,128)(2,1)} %wd_ref.1), custom_call_target="tpu_custom_call" | custom-call | flops 5637144576 | bytes 88080384 | tf_op jit(solution)/shard_map/pallas_call | solution.py:297
  47.8 1.5 %copy.9 = bf16[4,7168]{1,0:T(4,128)(2,1)} copy(bf16[4,7168]{1,0:T(4,128)(2,1)} %shard_map.73) | data formatting | bytes 114688

commit v4 on v3

--- a/solution.py
+++ b/solution.py
@@ -93,8 +93,6 @@
     for step in range(depth):
         for copy in gate_copies(jnp.int32(step)):
             copy.start()
-    for i in range(ring):
-        down_copy(i).start()
     table = slot_weights(id_ref[...], cw_ref[...], so_ref)
     high = table.astype(jnp.bfloat16).astype(jnp.float32)
     middle = (table - high).astype(jnp.bfloat16).astype(jnp.float32)
@@ -191,6 +189,8 @@
     pass_on(0)
     gather(0)
     lax.fori_loop(0, middle_slot, lambda s, _: slot_step(0, s), 0)
+    for i in range(ring):
+        down_copy(i).start()
     pass_on(1)
     lax.fori_loop(middle_slot, slots, lambda s, _: slot_step(0, s), 0)
     gather(1)

time: 49.5 us -> 54.6 us (1.10)
  Pallas kernels: 47.8 us -> 52.9 us
    pallas_call x1, Pallas kernels: 47.8 us -> 52.9 us  [body(): pl.pallas_call(functools.partial(kernel, n, n_dp, rows), out_shape=jax.Sh...]
where the time goes in v4:
time: 54.6 us; the launch traced here: 54.4 us
  Pallas kernels  52.9 us (97%)
  local copies, waits for them, and re-layouts  1.46 us (3%)
    pallas_call x1, Pallas kernels, body(): pl.pallas_call(functools.partial(kernel, n, n_dp, rows), out_shape=jax.Sh...  52.9 us
    unnamed x1, local copies, waits for them, and re-layouts  1.46 us

profile of v4, /device:TPU:0, one launch (start us, length us, event | category | flops | bytes accessed | tf_op | source)
XLA Modules:
  0.0 54.4 jit_solution(17246377404555809878)
XLA Ops:
  0.0 52.9 %shard_map.73 = bf16[4,7168]{1,0:T(4,128)(2,1)} custom-call(bf16[4,7168]{1,0:T(4,128)(2,1)} %t_ref.1, s32[4,8]{1,0:T(4,128)} %id_ref.1, f32[4,8]{1,0:T(4,128)} %cw_ref.1, s32[16]{0:T(128)} %so_ref.1, bf16[4,7168,512]{2,1,0:T(8,128)(2,1)} %wg_ref.1, bf16[4,7168,512]{2,1,0:T(8,128)(2,1)} %wu_ref.1, bf16[4,512,7168]{2,1,0:T(8,128)(2,1)} %wd_ref.1), custom_call_target="tpu_custom_call" | custom-call | flops 5637144576 | bytes 88080384 | tf_op jit(solution)/shard_map/pallas_call | solution.py:297
  52.9 1.5 %copy.9 = bf16[4,7168]{1,0:T(4,128)(2,1)} copy(bf16[4,7168]{1,0:T(4,128)(2,1)} %shard_map.73) | data formatting | bytes 114688
